TPU v7x, 32 devices: a whole 2x2x4 slice. The times are simulated.
32 devices in a mesh: dp: 8 (over y, x, core), batch: 4 (over z).
Axes of the slice: x: 2, y: 2, z: 4, core: 2. Of those that a mesh axis runs over, the one named last changes fastest.
Arguments:
- activations_in: float32 [32, 1024, 512], P(('dp', 'batch')), may hold values from -6 to 6
- gains: float32 [2, 2, 512], replicated, may hold values from 0.5 to 1.5
- shifts: float32 [2, 2, 512], replicated, may hold values from -2.5 to 2.5
- qkv_weights: bfloat16 [2, 3, 512, 512], replicated, may hold values from -0.25 to 0.25
- out_weights: bfloat16 [2, 512, 512], replicated, may hold values from -2 to 2
- up_weights: bfloat16 [2, 512, 2048], replicated, may hold values from -0.25 to 0.25
- up_bias: float32 [2, 2048], replicated, may hold values from -2.5 to 2.5
- down_weights: bfloat16 [2, 2048, 512], replicated, may hold values from -0.125 to 0.125
- down_bias: float32 [2, 512], replicated, may hold values from -2.5 to 2.5
- feature_maps: float32 [2, 8, 64, 256], replicated, may hold values from -4 to 4
- lengths: int32 [32, 6], P(('dp', 'batch')), may hold values from 18 to 146, as said below
- cotangent: float32 [32, 1024, 512], P(('dp', 'batch')), may hold values from -6 to 6
Outputs:
- activations_out: float32 [32, 1024, 512], P(('dp', 'batch'))
- input_grad: float32 [32, 1024, 512], P(('dp', 'batch'))
- gains_grad: float32 [2, 2, 512], P(None, None, 'batch')
- shifts_grad: float32 [2, 2, 512], P(None, None, 'batch')
- qkv_grad: float32 [2, 3, 512, 512], P(None, None, None, 'batch')
- out_grad: float32 [2, 512, 512], P(None, None, 'batch')
- up_grad: float32 [2, 512, 2048], P(None, None, 'batch')
- up_bias_grad: float32 [2, 2048], P(None, 'batch')
- down_grad: float32 [2, 2048, 512], P(None, None, 'batch')
- down_bias_grad: float32 [2, 512], P(None, 'batch')
Inputs may be any that keep to these rules, and one draw needn't show every extreme that they name: `lengths`: each of a row's 6 proteins has 18 to 146 tokens; in every row one protein has exactly 146 and another exactly 18; the remaining positions of the row are padding.
All inputs are finite; a program needn't handle non-finite values.
Results may differ from a plain program's by a relative error of at most 0.015.
The roundings to bfloat16 on the way count: a program that leaves them out, or rounds other values in their place, can miss the bound.
Values sent between devices are 32-bit elements; how exact they have to be, the bound alone decides.
No kernel may reach another device: no remote copies, remote signals or barrier semaphores. Data moves between devices by JAX's collectives and lax.ppermute only.
A program may use at most 384 MiB of HBM per device.

v0:
```python
import functools

import jax
import jax.numpy as jnp
from jax import lax
from jax.sharding import PartitionSpec as P

C = 256


highest = lax.Precision.HIGHEST


def layer_norm(values, gain_row, shift_row):
    average = jnp.mean(values, axis=-1, keepdims=True)
    centered = values - average
    spread = jnp.mean(centered * centered, axis=-1, keepdims=True)
    return centered * lax.rsqrt(spread + 1e-05) * gain_row + shift_row


def segments(lengths, length):
    bounds = jnp.cumsum(lengths, axis=-1)
    position = jnp.arange(length, dtype=jnp.int32)
    segment = jnp.sum((position[None, :, None] >= bounds[:, None, :]).astype(jnp.int32), axis=-1)
    in_protein = segment < lengths.shape[-1]
    return (segment, in_protein)


def features(values, feature_map):
    factor = values.shape[-1] ** (-0.25)
    projected = jnp.einsum("she,hem->shm", values, feature_map, precision=highest) * factor
    squares = jnp.sum(values * values, axis=-1, keepdims=True) * (factor * factor * 0.5)
    return jnp.exp(projected - squares) * feature_map.shape[-1] ** (-0.5)


def favor_row(queries, keys, values, segment, feature_map, block_len):
    length, head_count, head_dim = values.shape
    feat_count = feature_map.shape[-1]
    blocks = length // block_len
    phi_q = features(queries, feature_map).reshape(blocks, block_len, head_count, feat_count)
    phi_k = features(keys, feature_map).reshape(blocks, block_len, head_count, feat_count)
    value_blocks = values.reshape(blocks, block_len, head_count, head_dim)
    seg_blocks = segment.reshape(blocks, block_len)
    causal = jnp.arange(block_len)[:, None] >= jnp.arange(block_len)[None, :]

    def advance(carried_in, block_in):
        state_kv, state_k, previous = carried_in
        feat_q, feat_k, block_vals, seg_block = block_in
        same_doc = (seg_block[:, None] == seg_block[None, :]) & causal
        kernel = (
            jnp.einsum("thm,shm->hts", feat_q, feat_k, precision=highest)
            * same_doc.astype(feat_q.dtype)[None]
        )
        carried = (seg_block == previous).astype(feat_q.dtype)[:, None]
        numerator = jnp.einsum("hts,she->the", kernel, block_vals, precision=highest)
        numerator = numerator + carried[:, :, None] * jnp.einsum(
            "thm,hme->the", feat_q, state_kv, precision=highest
        )
        denominator = jnp.sum(kernel, axis=-1).T + carried * jnp.einsum(
            "thm,hm->th", feat_q, state_k, precision=highest
        )
        result = numerator / denominator[:, :, None]
        last_seg = seg_block[-1]
        carry_on = (last_seg == previous).astype(feat_q.dtype)
        member = (seg_block == last_seg).astype(feat_q.dtype)[:, None, None]
        kept_keys = feat_k * member
        state_kv = carry_on * state_kv + jnp.einsum(
            "shm,she->hme", kept_keys, block_vals, precision=highest
        )
        state_k = carry_on * state_k + jnp.sum(kept_keys, axis=0)
        return ((state_kv, state_k, last_seg), result)

    start = (
        jnp.zeros((head_count, feat_count, head_dim), values.dtype),
        jnp.zeros((head_count, feat_count), values.dtype),
        jnp.full((), -1, jnp.int32),
    )
    final_state, result = lax.scan(
        jax.checkpoint(advance), start, (phi_q, phi_k, value_blocks, seg_blocks)
    )
    return result.reshape(length, head_count * head_dim)


def favor(projected, feature_map, segment, block_len):
    head_count = feature_map.shape[0]
    row_count, length, model_dim = projected.shape[1:]
    stacked = projected.reshape(3, row_count, length, head_count, model_dim // head_count)
    per_row = functools.partial(favor_row, feature_map=feature_map, block_len=block_len)
    return jax.vmap(per_row)(stacked[0], stacked[1], stacked[2], segment)


def forward_layer(values, weights, feature_map, segment, pad_mask):
    gain_pair, shift_pair, qkv_mats, out_mat, up_mat, up_vec, down_mat, down_vec = weights
    normed_full, norm_pull = jax.vjp(layer_norm, values, gain_pair[0], shift_pair[0])
    normed = normed_full.astype(jnp.bfloat16)
    projected = jnp.einsum("rsd,jde->jrse", normed, qkv_mats, preferred_element_type=jnp.float32)
    attended, core_pull = jax.vjp(
        lambda stacked: favor(stacked, feature_map, segment, C), projected
    )
    attn_low = (attended * pad_mask).astype(jnp.bfloat16)
    mid_state = values + jnp.einsum(
        "rsd,de->rse", attn_low, out_mat, preferred_element_type=jnp.float32
    )
    normed_two_full, norm_two_pull = jax.vjp(layer_norm, mid_state, gain_pair[1], shift_pair[1])
    normed_two = normed_two_full.astype(jnp.bfloat16)
    pre_act = (
        jnp.einsum("rsd,df->rsf", normed_two, up_mat, preferred_element_type=jnp.float32) + up_vec
    )
    activated_full, gelu_pull = jax.vjp(functools.partial(jax.nn.gelu, approximate=False), pre_act)
    activated = activated_full.astype(jnp.bfloat16)
    result = (
        mid_state
        + jnp.einsum("rsf,fd->rsd", activated, down_mat, preferred_element_type=jnp.float32)
        + down_vec
    )
    kept = (norm_pull, normed, core_pull, attn_low, norm_two_pull, normed_two, gelu_pull, activated)
    return (result, kept)


def arrange(pieces, quarters):
    columns = []
    for piece in pieces:
        width = piece.shape[-1]
        columns.append(
            piece.reshape(-1, quarters, width // quarters).transpose(1, 0, 2).reshape(quarters, -1)
        )
    return jnp.concatenate(columns, axis=1)


def backward_layer(grad_out, kept, weights, pad_mask, quarters):
    gain_pair, shift_pair, qkv_mats, out_mat, up_mat, up_vec, down_mat, down_vec = weights
    norm_pull, normed, core_pull, attn_low, norm_two_pull, normed_two, gelu_pull, activated = kept
    grad_low = grad_out.astype(jnp.bfloat16)
    down_g = jnp.einsum("rsf,rsd->fd", activated, grad_low, preferred_element_type=jnp.float32)
    down_bias_g = jnp.sum(grad_low, axis=(0, 1), dtype=jnp.float32)
    act_g = jnp.einsum("rsd,fd->rsf", grad_low, down_mat, preferred_element_type=jnp.float32)
    (pre_g,) = gelu_pull(act_g)
    pre_low = pre_g.astype(jnp.bfloat16)
    up_g = jnp.einsum("rsd,rsf->df", normed_two, pre_low, preferred_element_type=jnp.float32)
    up_bias_g = jnp.sum(pre_low, axis=(0, 1), dtype=jnp.float32)
    normed_two_g = jnp.einsum("rsf,df->rsd", pre_low, up_mat, preferred_element_type=jnp.float32)
    mid_part, gain_two_g, shift_two_g = norm_two_pull(normed_two_g)
    mid_grad = grad_out + mid_part
    mid_low = mid_grad.astype(jnp.bfloat16)
    out_g = jnp.einsum("rsd,rse->de", attn_low, mid_low, preferred_element_type=jnp.float32)
    attended_g = (
        jnp.einsum("rse,de->rsd", mid_low, out_mat, preferred_element_type=jnp.float32) * pad_mask
    )
    (projected_g,) = core_pull(attended_g)
    proj_low = projected_g.astype(jnp.bfloat16)
    qkv_g = jnp.einsum("rsd,jrse->jde", normed, proj_low, preferred_element_type=jnp.float32)
    normed_g = jnp.einsum("jrse,jde->rsd", proj_low, qkv_mats, preferred_element_type=jnp.float32)
    in_part, gain_one_g, shift_one_g = norm_pull(normed_g)
    grad_in = mid_grad + in_part
    pieces = (
        jnp.stack([gain_one_g, gain_two_g]),
        jnp.stack([shift_one_g, shift_two_g]),
        qkv_g,
        out_g,
        up_g,
        up_bias_g,
        down_g,
        down_bias_g,
    )
    return (grad_in, arrange(pieces, quarters))


def total_sum(block):
    length = block.shape[1]
    quarter = lax.psum_scatter(block, "batch", scatter_dimension=0, tiled=True)[0]
    summed = lax.psum(quarter, "dp")
    return summed[:length]


def unpack(flat, shapes):
    pieces = []
    offset = 0
    for shape_one in shapes:
        count_one = 1
        for extent in shape_one:
            count_one = count_one * extent
        pieces.append(flat[offset : offset + count_one].reshape(shape_one))
        offset = offset + count_one
    return pieces


def per_device(
    activations_in,
    gains,
    shifts,
    qkv_weights,
    out_weights,
    up_weights,
    up_bias,
    down_weights,
    down_bias,
    feature_maps,
    lengths,
    cotangent,
):
    segment, in_protein = segments(lengths, activations_in.shape[1])
    pad_mask = in_protein.astype(jnp.float32)[..., None]
    layer_count = gains.shape[0]
    quarters = lax.axis_size("batch")
    params = (gains, shifts, qkv_weights, out_weights, up_weights, up_bias, down_weights, down_bias)
    shapes = [param.shape[1:-1] + (param.shape[-1] // quarters,) for param in params]
    values = activations_in
    saved = []
    for layer_id in range(layer_count):
        weights = tuple((param[layer_id] for param in params))
        values, kept = forward_layer(values, weights, feature_maps[layer_id], segment, pad_mask)
        saved.append(kept)
    grad = cotangent
    reduced = [None] * layer_count
    pending = []
    for layer_id in reversed(range(layer_count)):
        weights = tuple((param[layer_id] for param in params))
        grad, block = backward_layer(grad, saved[layer_id], weights, pad_mask, quarters)
        pending.insert(0, block)
    summed_all = total_sum(jnp.concatenate(pending, axis=1))
    reduced = jnp.split(summed_all, layer_count)
    parts = [unpack(reduced[layer_id], shapes) for layer_id in range(layer_count)]
    stacked = [
        jnp.stack([parts[layer_id][which] for layer_id in range(layer_count)])
        for which in range(len(shapes))
    ]
    return (
        values,
        grad,
        stacked[0],
        stacked[1],
        stacked[2],
        stacked[3],
        stacked[4],
        stacked[5],
        stacked[6],
        stacked[7],
    )


def solution(mesh):
    return jax.shard_map(
        per_device,
        mesh=mesh,
        in_specs=(
            P(("dp", "batch"), None, None),
            P(),
            P(),
            P(),
            P(),
            P(),
            P(),
            P(),
            P(),
            P(),
            P(("dp", "batch"), None),
            P(("dp", "batch"), None, None),
        ),
        out_specs=(
            P(("dp", "batch"), None, None),
            P(("dp", "batch"), None, None),
            P(None, None, "batch"),
            P(None, None, "batch"),
            P(None, None, None, "batch"),
            P(None, None, "batch"),
            P(None, None, "batch"),
            P(None, "batch"),
            P(None, None, "batch"),
            P(None, "batch"),
        ),
        check_vma=False,
    )
```

profile of v0, /device:TPU:0, one launch (start us, length us, event | category | flops | bytes accessed | tf_op | source)
XLA Modules:
  0.0 2409.2 jit_solution(5796961404493727900)
XLA Ops:
  24.5 12.5 fusion.385
  42.7 12.8 fusion.384
  69.3 96.1 %while.92 = (s32[]{:T(128)}, f32[1,8,256,64]{2,3,1,0:T(8,128)S(1)}, f32[1,8,256]{2,1,0:T(8,128)S(1)}, s32[1]{0:T(128)}, f32[4,1,256,8,64]{2,4,3,1,0:T(8,128)}, /...) while((s32[]{:T(128)}, f32[1,8,256,64]{2,3,1,0:T(8,128)S(1)}, ...), condition=%wide.region_9.10_spmd.clone, body=%wide.region_6.9_spmd.clone.sunk | while | flops 2829329408 | bytes 22938836 | solution.py:78
  171.6 24.2 %multiply_convert_fusion.1 = (bf16[1024,2048]{1,0:T(8,128)(2,1)S(1)}, f32[1024,2048]{1,0:T(8,128)}, f32[1024,2048]{1,0:T(8,128)}) fusion(f32[2048]{0:T(1024)S(1)} %bitcast.1676, bf16[2,512,2048]{2,1,0:T(8,128)(2,1)S(1)} %copy-done.150, f32[512]{0:T(512)S(1)} %bitcast.1709, f32[512]{0:T(512)S(1)} %bitcast.1692, f32[1024]{0:T(1024)S(1)} %fusion.503, ...), kind=kOutput, calls=%fused_computation.407 | convolution fusion | flops 2288517120 | bytes 25186304 | tf_op jit(solution)/shard_map/rsd,df->rsf/dot_general | solution.py:107
  209.0 12.5 fusion.387
  227.2 12.6 fusion.386
  253.5 95.4 %while.93 = (s32[]{:T(128)}, f32[1,8,256,64]{2,3,1,0:T(8,128)S(1)}, f32[1,8,256]{2,1,0:T(8,128)S(1)}, s32[1]{0:T(128)}, f32[4,1,256,8,64]{2,4,3,1,0:T(8,128)}, /...) while((s32[]{:T(128)}, f32[1,8,256,64]{2,3,1,0:T(8,128)S(1)}, ...), condition=%wide.region_19.20_spmd.clone, body=%wide.region_16.19_spmd.clone.sunk | while | flops 2829329408 | bytes 22938836 | solution.py:78
  362.7 23.6 convert_reduce_fusion
  409.9 290.7 %while.94 = (s32[]{:T(128)}, f32[1,8,256,64]{2,3,1,0:T(8,128)}, f32[1,8,256]{2,1,0:T(8,128)S(1)}, f32[4,1,256,8,256]{2,4,3,1,0:T(8,128)}, f32[4,1,256,8,256]{2,4...) while((s32[]{:T(128)}, f32[1,8,256,64]{2,3,1,0:T(8,128)}, ...), condition=%wide.region_27.28_spmd.clone, body=%wide.region_24.27_spmd.clone.sunk | while | flops 8075756544 | bytes 120993248 | solution.py:78
  449.7 12.3 dynamic_update_slice.131
  516.5 12.3 dynamic_update_slice.131
  583.2 12.3 dynamic_update_slice.131
  650.0 12.3 dynamic_update_slice.131
  717.5 9.6 fusion.523
  741.9 9.3 fusion.524
  754.7 11.0 fusion.405
  784.4 13.1 convert_reduce_fusion.1
  823.4 287.1 %while.95 = (s32[]{:T(128)}, f32[1,8,256,64]{2,3,1,0:T(8,128)}, f32[1,8,256]{2,1,0:T(8,128)S(1)}, f32[4,1,256,8,256]{2,4,3,1,0:T(8,128)}, f32[4,1,256,8,256]{2,4...) while((s32[]{:T(128)}, f32[1,8,256,64]{2,3,1,0:T(8,128)}, ...), condition=%wide.region_37.38_spmd.clone, body=%wide.region_34.37_spmd.clone.sunk | while | flops 8075756544 | bytes 120993248 | solution.py:78
  863.9 12.3 dynamic_update_slice.134
  931.3 12.3 dynamic_update_slice.134
  998.7 12.3 dynamic_update_slice.134
  1066.1 12.3 dynamic_update_slice.134
  1144.1 17.5 fusion.520
  1165.0 10.9 fusion.403
  1206.3 22.8 fusion.323
  1245.8 21.5 fusion.318
  1317.8 10.0 multiply_convert_fusion
  1339.0 10.3 bitcast_dynamic-update-slice_fusion.5
  1361.6 10.3 bitcast_dynamic-update-slice_fusion.4
  1373.7 836.6 %all-reduce.12.cloned.1.call-done = f32[4,1575168]{1,0:T(4,128)} async-done(((f32[4,1575168]{1,0:T(4,128)}), f32[4,1575168]{1,0:T(4,128)}) %all-reduce.12.cloned.1.call-update) | async-done | bytes 25202704
  2210.3 70.0 %dynamic-slice_reduce_fusion = f32[1575168]{0:T(1024)} fusion(f32[4,1575168]{1,0:T(4,128)} %all-reduce.12.cloned.1.call-done, u32[]{:T(128)} %bitcast.385), kind=kLoop, calls=%fused_computation.430 | loop fusion | bytes 12601348 | tf_op jit(solution)/shard_map/squeeze | solution.py:170
  2298.6 85.6 %all-reduce.10.cloned.1.call-done = f32[1575168]{0:T(1024)} async-done(((f32[1575168]{0:T(1024)}), f32[1575168]{0:T(1024)}) %all-reduce.10.cloned.1.call-update) | async-done | bytes 6300688 | tf_op jit(solution)/shard_map/psum | solution.py:171
  (1014 shorter events, 990.7 us)
Async XLA Ops:
  7.2 2203.1 %all-reduce.12.cloned.1.call-start = ((), (), s32[]{:S(2)}) async-start(), calls=%async_computation.1 | async-start | bytes 50405376
  9.3 159.3 %copy-start.17 = (f32[1,1024,512]{1,2,0:T(8,128)}, f32[1,1024,512]{1,2,0:T(8,128)S(1)}, u32[]{:S(2)}) copy-start(f32[1,1024,512]{1,2,0:T(8,128)S(1)} %copy.242) | copy-start | bytes 6291460
  12.8 158.1 %copy-start.129 = (f32[1,1,512]{2,1,0:T(1,128)}, f32[1,1,512]{2,1,0:T(1,128)S(1)}, u32[]{:S(2)}) copy-start(f32[1,1,512]{2,1,0:T(1,128)S(1)} %get-tuple-element.1427) | copy-start | bytes 6148
  12.8 185.9 %copy-start.118 = (f32[1,1,512]{2,1,0:T(1,128)}, f32[1,1,512]{2,1,0:T(1,128)S(1)}, u32[]{:S(2)}) copy-start(f32[1,1,512]{2,1,0:T(1,128)S(1)} %get-tuple-element.1429) | copy-start | bytes 6148
  13.4 157.6 %copy-start.142 = (f32[1,1,512]{2,1,0:T(1,128)}, f32[1,1,512]{2,1,0:T(1,128)S(1)}, u32[]{:S(2)}) copy-start(f32[1,1,512]{2,1,0:T(1,128)S(1)} %get-tuple-element.1431) | copy-start | bytes 6148
  13.4 185.3 %copy-start.146 = (f32[1,1,512]{2,1,0:T(1,128)}, f32[1,1,512]{2,1,0:T(1,128)S(1)}, u32[]{:S(2)}) copy-start(f32[1,1,512]{2,1,0:T(1,128)S(1)} %get-tuple-element.1433) | copy-start | bytes 6148
  24.4 12.5 copy-start.72
  42.7 12.8 copy-start.74
  66.2 99.3 %copy-start.95 = (f32[1024]{0:T(1024)}, f32[1024]{0:T(1024)S(1)}, u32[]{:S(2)}) copy-start(f32[1024]{0:T(1024)S(1)} %compare_convert_fusion.9) | copy-start | bytes 12292
  169.4 26.5 %copy-start.30 = (f32[1,1024,512]{1,2,0:T(8,128)}, f32[1,1024,512]{1,2,0:T(8,128)S(1)}, u32[]{:S(2)}) copy-start(f32[1,1024,512]{1,2,0:T(8,128)S(1)} %get-tuple-element.1441) | copy-start | bytes 6291460
  169.4 26.4 %copy-start.106 = (f32[1024]{0:T(1024)}, f32[1024]{0:T(1024)S(1)}, u32[]{:S(2)}) copy-start(f32[1024]{0:T(1024)S(1)} %broadcast_multiply_fusion.10) | copy-start | bytes 12292
  170.3 25.5 %copy-start.122 = (f32[1024]{0:T(1024)}, f32[1024]{0:T(1024)S(1)}, u32[]{:S(2)}) copy-start(f32[1024]{0:T(1024)S(1)} %fusion.503) | copy-start | bytes 12292
  170.3 25.5 %copy-start.113 = (f32[1,2048]{1,0:T(1,128)}, f32[1,2048]{1,0:T(1,128)S(1)}, u32[]{:S(2)}) copy-start(f32[1,2048]{1,0:T(1,128)S(1)} %get-tuple-element.1425) | copy-start | bytes 24580
  170.3 192.3 %copy-start.85 = (f32[1,2048]{1,0:T(1,128)}, f32[1,2048]{1,0:T(1,128)S(1)}, u32[]{:S(2)}) copy-start(f32[1,2048]{1,0:T(1,128)S(1)} %get-tuple-element.1424) | copy-start | bytes 24580
  171.6 24.2 %copy-start.153 = (bf16[2,2048,512]{2,1,0:T(8,128)(2,1)S(1)}, bf16[2,2048,512]{2,1,0:T(8,128)(2,1)}, u32[]{:S(2)}) copy-start(bf16[2,2048,512]{2,1,0:T(8,128)(2,1)} %param.27) | copy-start | bytes 12582916
  198.3 154.3 %copy-start.21 = (f32[1,1024,512]{1,2,0:T(8,128)}, f32[1,1024,512]{1,2,0:T(8,128)S(1)}, u32[]{:S(2)}) copy-start(f32[1,1024,512]{1,2,0:T(8,128)S(1)} %get-tuple-element.1444) | copy-start | bytes 6291460
  209.0 12.5 copy-start.76
  227.2 12.7 copy-start.78
  353.4 36.1 %copy-start.109 = (f32[1024]{0:T(1024)}, f32[1024]{0:T(1024)S(1)}, u32[]{:S(2)}) copy-start(f32[1024]{0:T(1024)S(1)} %broadcast_multiply_fusion.8) | copy-start | bytes 12292
  354.7 34.9 %copy-start.125 = (f32[1024]{0:T(1024)}, f32[1024]{0:T(1024)S(1)}, u32[]{:S(2)}) copy-start(f32[1024]{0:T(1024)S(1)} %fusion.505) | copy-start | bytes 12292
  357.0 33.2 %copy-start.26 = (f32[1,1024,512]{1,2,0:T(8,128)}, f32[1,1024,512]{1,2,0:T(8,128)S(1)}, u32[]{:S(2)}) copy-start(f32[1,1024,512]{1,2,0:T(8,128)S(1)} %copy.250) | copy-start | bytes 6291460
  362.6 23.7 copy-start.19
  362.6 23.7 copy-start.33
  362.6 23.6 copy-start.151
  784.3 13.2 copy-start.67
  784.3 19.3 copy-start.35
  784.3 13.2 copy-start.31
  784.3 13.2 copy-start.107
  784.4 13.2 copy-start.123
  784.4 13.1 copy-start.130
  784.4 13.1 copy-start.152
  1372.5 1011.7 %all-reduce.10.cloned.1.call-start = ((), (), s32[]{:S(2)}) async-start(), calls=%async_computation | async-start | bytes 12607488 | tf_op jit(solution)/shard_map/psum | solution.py:171
  (189 other events, 867.2 us)
Sparse Core Ops, SparseCore 0:
  1372.6 837.6 all-reduce.11
  2280.4 103.7 all-reduce.9
where the time goes:
time: 2420 us; the launch traced here: 2410 us
  waiting for transfers between devices  922 us (38%)
  matrix products  641 us (26%)
  local copies, waits for them, and re-layouts  542 us (22%)
  other arithmetic  221 us (9%)
  loops' own time  66.7 us (3%)
    unnamed x3, waiting for transfers between devices  837 us
    dynamic_update_slice x40, local copies, waits for them, and re-layouts, favor_row(): lax.scan(jax.checkpoint(advance), start, (phi_q, phi_k, value_blocks, seg...  159 us
    dot_general x32, matrix products, advance(): jnp.einsum('thm,shm->hts', feat_q, feat_k, precision=highest)  114 us
    dot_general x32, matrix products, advance(): jnp.einsum('thm,hme->the', feat_q, state_kv, precision=highest)  108 us
    unnamed x342, local copies, waits for them, and re-layouts  107 us
    dot_general x8, matrix products, features(): jnp.einsum('she,hem->shm', values, feature_map, precision=highest) * factor  88.8 us
    psum x1, waiting for transfers between devices, total_sum(): summed = lax.psum(quarter, 'dp')  85.6 us
    dot_general x24, matrix products, advance(): jnp.einsum('shm,she->hme', kept_keys, block_vals, precision=highest)  84.8 us
  transfers between devices with their start and end apart: 2, of which 2 were waited for; matrix products, arithmetic and copies ran while one was open for 1% of the time, Pallas kernels for 0%

commit v1 on v0

v1 whole, which is shorter than its diff:
```python
import functools
import math

import jax
import jax.numpy as jnp
from jax import lax
from jax.experimental import pallas as pl
from jax.experimental.pallas import tpu as pltpu
from jax.sharding import PartitionSpec as P

BLOCK = 256
BLOCKS = 3
LIVE = BLOCK * BLOCKS
REACH = 160
LANES = 128
NDOC = 6
MIB = 1 << 20
F32 = jnp.float32
BF16 = jnp.bfloat16
LOG2E = 1.4426950408889634
NT = (((1,), (1,)), ((), ()))
TN = (((0,), (0,)), ((), ()))


def dot(a, b):
    return jnp.dot(a, b, preferred_element_type=F32)


def dot_nt(a, b):
    return lax.dot_general(a, b, NT, preferred_element_type=F32)


def dot_tn(a, b):
    return lax.dot_general(a, b, TN, preferred_element_type=F32)


def params_for(mib):
    return pltpu.CompilerParams(vmem_limit_bytes=mib * MIB)


def cost(flops, traffic, transcendentals=0):
    return pl.CostEstimate(flops=int(flops), bytes_accessed=int(traffic), transcendentals=int(transcendentals))


def normalize(values):
    centered = values - jnp.mean(values, axis=-1, keepdims=True)
    rstd = lax.rsqrt(jnp.mean(centered * centered, axis=-1, keepdims=True) + 1e-05)
    return centered * rstd, rstd


def norm_pull(grad, gain, unit, rstd):
    p = grad * gain
    return rstd * (p - jnp.mean(p, axis=-1, keepdims=True) - unit * jnp.mean(p * unit, axis=-1, keepdims=True))


def split_two(values):
    high = values.astype(BF16)
    return high, (values - high.astype(F32)).astype(BF16)


def protein_ids(len_ref, position):
    bound = jnp.int32(0)
    ids = jnp.zeros(position.shape, jnp.int32)
    for j in range(NDOC):
        bound = bound + len_ref[j]
        ids = ids + (position >= bound).astype(jnp.int32)
    return ids


def token_count(len_ref):
    total = jnp.int32(0)
    for j in range(NDOC):
        total = total + len_ref[j]
    return total


def pair_mask(len_ref, shape, first_row, first_col, causal_rows):
    rows = lax.broadcasted_iota(jnp.int32, shape, 0) + first_row
    cols = lax.broadcasted_iota(jnp.int32, shape, 1) + first_col
    same = protein_ids(len_ref, rows) == protein_ids(len_ref, cols)
    ordered = (rows >= cols) if causal_rows else (cols >= rows)
    return jnp.where(same & ordered, 1.0, 0.0).astype(BF16)


def fill_masks(len_ref, own_ref, before_ref, causal_rows):
    for b in range(BLOCKS):
        own_ref[b] = pair_mask(len_ref, (BLOCK, BLOCK), b * BLOCK, b * BLOCK, causal_rows)
    for b in range(1, BLOCKS):
        if causal_rows:
            before_ref[b - 1] = pair_mask(len_ref, (REACH, BLOCK), b * BLOCK, (b - 1) * BLOCK, True)
        else:
            before_ref[b - 1] = pair_mask(len_ref, (REACH, BLOCK), b * BLOCK - REACH, b * BLOCK, False)


def attn_fwd_body(len_ref, x_ref, gain_ref, shift_ref, w_ref, fm_ref, normed_ref, phi_q_ref, phi_k_ref, uq_ref, uk_ref,
                  v_ref, att_ref, rden_ref, low_ref, proj_ref, own_ref, before_ref, num_ref):
    step = pl.program_id(0)

    @pl.when(step == 0)
    def _():
        fill_masks(len_ref, own_ref, before_ref, True)
        for b in range(BLOCKS):
            rows = pl.ds(b * BLOCK, BLOCK)
            unit, _ = normalize(x_ref[rows, :])
            normed_ref[rows, :] = (unit * gain_ref[...] + shift_ref[...]).astype(BF16)
        for j in range(3):
            for half in range(2):
                got = dot(normed_ref[...], w_ref[j, :, half * 256 : half * 256 + 256])
                proj_ref[j, 2 * half] = got[:, :LANES]
                proj_ref[j, 2 * half + 1] = got[:, LANES:]

    lane = lax.broadcasted_iota(jnp.int32, (BLOCK, LANES), 1) < 64
    uq_ref[0] = proj_ref[0, step]
    uk_ref[0] = proj_ref[1, step]
    v_ref[0] = proj_ref[2, step].astype(BF16)
    for which, phi_ref in ((0, phi_q_ref), (1, phi_k_ref)):
        for head in range(2):
            high, low = split_two(fm_ref[head] * (64.0 ** (-0.25) * LOG2E))
            stacked = jnp.concatenate([high, low, high, low], axis=0)
            for b in range(BLOCKS):
                rows = pl.ds(b * BLOCK, BLOCK)
                u = proj_ref[which, step, rows, :]
                turned = pltpu.roll(u, 64, 1)
                twice = jnp.where(lane, u, turned) if head == 0 else jnp.where(lane, turned, u)
                squares = jnp.sum(twice * twice, axis=-1, keepdims=True) * (LOG2E / 32.0) + 4.0
                u_high, u_low = split_two(twice)
                projected = dot(jnp.concatenate([u_high, u_low], axis=1), stacked)
                phi_ref[head, rows, :] = jnp.exp2(projected - squares).astype(BF16)
    ones = jnp.ones((BLOCK, LANES), BF16)
    for b in range(BLOCKS):
        rows = pl.ds(b * BLOCK, BLOCK)
        v_now = jnp.concatenate([v_ref[0, rows, :], ones], axis=1)
        for head in range(2):
            weights = dot_nt(phi_q_ref[head, rows, :], phi_k_ref[head, rows, :]).astype(BF16) * own_ref[b]
            num_ref[head] = dot(weights, v_now)
            if b > 0:
                earlier = pl.ds((b - 1) * BLOCK, BLOCK)
                v_before = jnp.concatenate([v_ref[0, earlier, :], ones], axis=1)
                weights = dot_nt(phi_q_ref[head, pl.ds(b * BLOCK, REACH), :], phi_k_ref[head, earlier, :])
                num_ref[head, :REACH, :] += dot(weights.astype(BF16) * before_ref[b - 1], v_before)
        rden = 1.0 / jnp.where(lane, num_ref[0, :, LANES:], num_ref[1, :, LANES:])
        attended = jnp.where(lane, num_ref[0, :, :LANES], num_ref[1, :, :LANES]) * rden
        position = lax.broadcasted_iota(jnp.int32, (BLOCK, LANES), 0) + b * BLOCK
        attended = jnp.where(position < token_count(len_ref), attended, 0.0)
        rden_ref[0, rows, :] = rden
        att_ref[0, rows, :] = attended
        low_ref[rows, :] = attended.astype(BF16)


def attn_fwd(lengths, x, gain, shift, w, fm):
    width = x.shape[1]
    heads = fm.shape[0]
    pairs = heads // 2
    per_pair = pl.BlockSpec((1, LIVE, LANES), lambda p, *_: (p, 0, 0))
    per_head = pl.BlockSpec((2, LIVE, 256), lambda p, *_: (p, 0, 0))
    whole = lambda *shape: pl.BlockSpec(shape, lambda p, *_: (0,) * len(shape))
    return pl.pallas_call(
        attn_fwd_body,
        grid_spec=pltpu.PrefetchScalarGridSpec(
            num_scalar_prefetch=1,
            grid=(pairs,),
            in_specs=[
                whole(LIVE, width),
                whole(1, width),
                whole(1, width),
                whole(3, width, width),
                pl.BlockSpec((2, 64, 256), lambda p, *_: (p, 0, 0)),
            ],
            out_specs=[
                whole(LIVE, width),
                per_head,
                per_head,
                per_pair,
                per_pair,
                per_pair,
                per_pair,
                per_pair,
                pl.BlockSpec((LIVE, LANES), lambda p, *_: (0, p)),
            ],
            scratch_shapes=[
                pltpu.VMEM((3, pairs, LIVE, LANES), F32),
                pltpu.VMEM((BLOCKS, BLOCK, BLOCK), BF16),
                pltpu.VMEM((BLOCKS - 1, REACH, BLOCK), BF16),
                pltpu.VMEM((2, BLOCK, 256), F32),
            ],
        ),
        out_shape=[
            jax.ShapeDtypeStruct((LIVE, width), BF16),
            jax.ShapeDtypeStruct((heads, LIVE, 256), BF16),
            jax.ShapeDtypeStruct((heads, LIVE, 256), BF16),
            jax.ShapeDtypeStruct((pairs, LIVE, LANES), F32),
            jax.ShapeDtypeStruct((pairs, LIVE, LANES), F32),
            jax.ShapeDtypeStruct((pairs, LIVE, LANES), BF16),
            jax.ShapeDtypeStruct((pairs, LIVE, LANES), F32),
            jax.ShapeDtypeStruct((pairs, LIVE, LANES), F32),
            jax.ShapeDtypeStruct((LIVE, width), BF16),
        ],
        compiler_params=params_for(48),
        cost_estimate=cost(1.2e10, 2e7, 4e6),
        name="attn_forward",
    )(lengths, x, gain, shift, w, fm)


def ff_fwd_body(x_ref, low_ref, wo_ref, gain_ref, shift_ref, up_ref, up_bias_ref, down_ref, down_bias_ref,
                out_ref, mid_ref, normed_ref, act_ref, slope_ref):
    step = pl.program_id(0)
    mid_ref[...] = x_ref[...]

    @pl.when(step < BLOCKS)
    def _():
        mid_ref[...] += dot(low_ref[...], wo_ref[...])

    mid = mid_ref[...]
    unit, _ = normalize(mid)
    normed = (unit * gain_ref[...] + shift_ref[...]).astype(BF16)
    normed_ref[...] = normed
    total = mid + down_bias_ref[...]
    hidden = up_ref.shape[1]
    for first in range(0, hidden, 512):
        cols = slice(first, first + 512)
        pre = dot(normed, up_ref[:, cols]) + up_bias_ref[:, cols]
        lifted = 0.5 + 0.5 * lax.erf(pre * math.sqrt(0.5))
        slope_ref[:, cols] = lifted + pre * (jnp.exp2(pre * pre * (-0.5 * LOG2E)) * (1.0 / math.sqrt(2.0 * math.pi)))
        act = (pre * lifted).astype(BF16)
        act_ref[:, cols] = act
        total = total + dot(act, down_ref[cols, :])
    out_ref[...] = total


def ff_fwd(x, low, wo, gain, shift, up, up_bias, down, down_bias):
    length, width = x.shape
    hidden = up.shape[1]
    rows = lambda n: pl.BlockSpec((BLOCK, n), lambda i: (i, 0))
    whole = lambda *shape: pl.BlockSpec(shape, lambda i: (0,) * len(shape))
    return pl.pallas_call(
        ff_fwd_body,
        grid=(length // BLOCK,),
        in_specs=[
            rows(width),
            pl.BlockSpec((BLOCK, width), lambda i: (jnp.minimum(i, BLOCKS - 1), 0)),
            whole(width, width),
            whole(1, width),
            whole(1, width),
            whole(width, hidden),
            whole(1, hidden),
            whole(hidden, width),
            whole(1, width),
        ],
        out_specs=[rows(width), rows(width), rows(width), rows(hidden), rows(hidden)],
        out_shape=[
            jax.ShapeDtypeStruct((length, width), F32),
            jax.ShapeDtypeStruct((length, width), F32),
            jax.ShapeDtypeStruct((length, width), BF16),
            jax.ShapeDtypeStruct((length, hidden), BF16),
            jax.ShapeDtypeStruct((length, hidden), F32),
        ],
        compiler_params=params_for(48),
        cost_estimate=cost(2 * length * width * (width + 2 * hidden), 3e7, 2 * length * hidden),
        name="ff_forward",
    )(x, low, wo, gain, shift, up, up_bias, down, down_bias)


def ff_bwd_body(g_ref, slope_ref, mid_ref, gain_ref, up_ref, down_ref, wo_ref,
                g_low_ref, pre_low_ref, mid_g_ref, mid_low_ref, att_g_ref, small_ref, up_bias_ref):
    step = pl.program_id(0)

    @pl.when(step == 0)
    def _():
        small_ref[...] = jnp.zeros_like(small_ref)
        up_bias_ref[...] = jnp.zeros_like(up_bias_ref)

    grad = g_ref[...]
    g_low = grad.astype(BF16)
    g_low_ref[...] = g_low
    back = jnp.zeros(grad.shape, F32)
    hidden = up_ref.shape[1]
    for first in range(0, hidden, 512):
        cols = slice(first, first + 512)
        pre_low = (dot_nt(g_low, down_ref[cols, :]) * slope_ref[:, cols]).astype(BF16)
        pre_low_ref[:, cols] = pre_low
        up_bias_ref[:, cols] += jnp.sum(pre_low.astype(F32), axis=0, keepdims=True)
        back = back + dot_nt(pre_low, up_ref[:, cols])
    unit, rstd = normalize(mid_ref[...])
    mid_g = grad + norm_pull(back, gain_ref[...], unit, rstd)
    mid_g_ref[...] = mid_g
    mid_low = mid_g.astype(BF16)
    mid_low_ref[...] = mid_low
    small_ref[0:1, :] += jnp.sum(back * unit, axis=0, keepdims=True)
    small_ref[1:2, :] += jnp.sum(back, axis=0, keepdims=True)
    small_ref[2:3, :] += jnp.sum(g_low.astype(F32), axis=0, keepdims=True)

    @pl.when(step < BLOCKS)
    def _():
        att_g_ref[...] = dot_nt(mid_low, wo_ref[...])


def ff_bwd(grad, slope, mid, gain, up, down, wo):
    length, width = grad.shape
    hidden = up.shape[1]
    rows = lambda n: pl.BlockSpec((BLOCK, n), lambda i: (i, 0))
    whole = lambda *shape: pl.BlockSpec(shape, lambda i: (0,) * len(shape))
    return pl.pallas_call(
        ff_bwd_body,
        grid=(length // BLOCK,),
        in_specs=[
            rows(width),
            rows(hidden),
            rows(width),
            whole(1, width),
            whole(width, hidden),
            whole(hidden, width),
            whole(width, width),
        ],
        out_specs=[
            rows(width),
            rows(hidden),
            rows(width),
            rows(width),
            pl.BlockSpec((BLOCK, width), lambda i: (jnp.minimum(i, BLOCKS - 1), 0)),
            whole(8, width),
            whole(1, hidden),
        ],
        out_shape=[
            jax.ShapeDtypeStruct((length, width), BF16),
            jax.ShapeDtypeStruct((length, hidden), BF16),
            jax.ShapeDtypeStruct((length, width), F32),
            jax.ShapeDtypeStruct((length, width), BF16),
            jax.ShapeDtypeStruct((LIVE, width), F32),
            jax.ShapeDtypeStruct((8, width), F32),
            jax.ShapeDtypeStruct((1, hidden), F32),
        ],
        compiler_params=params_for(48),
        cost_estimate=cost(2 * length * width * (width + 2 * hidden), 3e7),
        name="ff_backward",
    )(grad, slope, mid, gain, up, down, wo)


def attn_bwd_body(len_ref, att_g_ref, att_ref, rden_ref, phi_q_ref, phi_k_ref, uq_ref, uk_ref, v_ref, fm_ref,
                  dq_ref, dk_ref, dv_ref, own_ref, before_ref, own_t_ref, before_t_ref,
                  x_ref, y_ref, dn_ref, d_phi_q, d_phi_k, d_v, raw_ref):
    step = pl.program_id(0)

    @pl.when(step == 0)
    def _():
        fill_masks(len_ref, own_ref, before_ref, True)
        fill_masks(len_ref, own_t_ref, before_t_ref, False)

    lane = lax.broadcasted_iota(jnp.int32, (BLOCK, LANES), 1) < 64
    one = jnp.ones((BLOCK, LANES), BF16)
    for b in range(BLOCKS):
        rows = pl.ds(b * BLOCK, BLOCK)
        position = lax.broadcasted_iota(jnp.int32, (BLOCK, LANES), 0) + b * BLOCK
        dn = jnp.where(position < token_count(len_ref), att_g_ref[rows, :] * rden_ref[0, rows, :], 0.0)
        turned = pltpu.roll(-(dn * att_ref[0, rows, :]), 64, 1)
        dn_ref[rows, :] = dn.astype(BF16)
        v_low = v_ref[0, rows, :]
        for head in range(2):
            first = lane if head == 0 else jnp.logical_not(lane)
            high, low = split_two(jnp.where(first, dn, turned))
            x_ref[head, rows, :] = jnp.concatenate([high, low], axis=1)
            y = jnp.where(first, v_low.astype(F32), 1.0).astype(BF16)
            y_ref[head, rows, :] = jnp.concatenate([y, y], axis=1)
    for head in range(2):
        for b in range(BLOCKS):
            rows = pl.ds(b * BLOCK, BLOCK)
            x, y = x_ref[head, rows, :], y_ref[head, rows, :]
            phi_q, phi_k = phi_q_ref[head, rows, :], phi_k_ref[head, rows, :]
            d_kernel = dot_nt(x, y).astype(BF16) * own_ref[b]
            d_phi_q[rows, :] = dot(d_kernel, phi_k)
            d_kernel_t = dot_nt(y, x).astype(BF16) * own_t_ref[b]
            d_phi_k[rows, :] = dot(d_kernel_t, phi_q)
            kernel_t = dot_nt(phi_k, phi_q).astype(BF16) * own_t_ref[b]
            d_v[head, rows, :] = dot(kernel_t, dn_ref[rows, :])
            if b > 0:
                earlier = pl.ds((b - 1) * BLOCK, BLOCK)
                top = pl.ds(b * BLOCK, REACH)
                bottom = pl.ds(b * BLOCK - REACH, REACH)
                d_kernel = dot_nt(x_ref[head, top, :], y_ref[head, earlier, :]).astype(BF16) * before_ref[b - 1]
                d_phi_q[top, :] += dot(d_kernel, phi_k_ref[head, earlier, :])
                d_kernel_t = dot_nt(y_ref[head, bottom, :], x).astype(BF16) * before_t_ref[b - 1]
                d_phi_k[bottom, :] += dot(d_kernel_t, phi_q)
                kernel_t = dot_nt(phi_k_ref[head, bottom, :], phi_q).astype(BF16) * before_t_ref[b - 1]
                d_v[head, bottom, :] += dot(kernel_t, dn_ref[rows, :])
        high, low = split_two(fm_ref[head])
        stacked = jnp.concatenate([high, low, jnp.ones((LANES, 256), BF16)], axis=0)
        for which, d_phi, phi_ref in ((0, d_phi_q, phi_q_ref), (1, d_phi_k, phi_k_ref)):
            for b in range(BLOCKS):
                rows = pl.ds(b * BLOCK, BLOCK)
                d_projected = (d_phi[rows, :] * phi_ref[head, rows, :].astype(F32)).astype(BF16)
                raw_ref[which, head, rows, :] = dot_nt(d_projected, stacked)
    for b in range(BLOCKS):
        rows = pl.ds(b * BLOCK, BLOCK)
        for which, u_ref, out_ref in ((0, uq_ref, dq_ref), (1, uk_ref, dk_ref)):
            parts = []
            for head in range(2):
                raw = raw_ref[which, head, rows, :LANES]
                parts.append(raw + pltpu.roll(raw, 64, 1))
            along = jnp.where(lane, parts[0], parts[1])
            total = jnp.where(lane, raw_ref[which, 0, rows, LANES:], raw_ref[which, 1, rows, LANES:])
            grad = along * (64.0 ** (-0.25)) - u_ref[0, rows, :] * total * 0.125
            out_ref[rows, :] = grad.astype(BF16)
        dv_ref[rows, :] = jnp.where(lane, d_v[0, rows, :], d_v[1, rows, :]).astype(BF16)


def attn_bwd(lengths, att_g, att, rden, phi_q, phi_k, uq, uk, v, fm):
    heads = fm.shape[0]
    pairs = heads // 2
    width = att_g.shape[1]
    per_pair = pl.BlockSpec((1, LIVE, LANES), lambda p, *_: (p, 0, 0))
    per_head = pl.BlockSpec((2, LIVE, 256), lambda p, *_: (p, 0, 0))
    columns = pl.BlockSpec((LIVE, LANES), lambda p, *_: (0, p))
    return pl.pallas_call(
        attn_bwd_body,
        grid_spec=pltpu.PrefetchScalarGridSpec(
            num_scalar_prefetch=1,
            grid=(pairs,),
            in_specs=[columns, per_pair, per_pair, per_head, per_head, per_pair, per_pair, per_pair,
                      pl.BlockSpec((2, 64, 256), lambda p, *_: (p, 0, 0))],
            out_specs=[columns] * 3,
            scratch_shapes=[
                pltpu.VMEM((BLOCKS, BLOCK, BLOCK), BF16),
                pltpu.VMEM((BLOCKS - 1, REACH, BLOCK), BF16),
                pltpu.VMEM((BLOCKS, BLOCK, BLOCK), BF16),
                pltpu.VMEM((BLOCKS - 1, REACH, BLOCK), BF16),
                pltpu.VMEM((2, LIVE, 256), BF16),
                pltpu.VMEM((2, LIVE, 256), BF16),
                pltpu.VMEM((LIVE, LANES), BF16),
                pltpu.VMEM((LIVE, 256), F32),
                pltpu.VMEM((LIVE, 256), F32),
                pltpu.VMEM((2, LIVE, LANES), F32),
                pltpu.VMEM((2, 2, LIVE, 256), F32),
            ],
        ),
        out_shape=[jax.ShapeDtypeStruct((LIVE, width), BF16)] * 3,
        compiler_params=params_for(48),
        cost_estimate=cost(3e10, 2e7),
        name="attn_backward",
    )(lengths, att_g, att, rden, phi_q, phi_k, uq, uk, v, fm)


def input_bwd_body(dq_ref, dk_ref, dv_ref, w_ref, x_ref, gain_ref, mid_g_ref, out_ref, small_ref):
    step = pl.program_id(0)

    @pl.when(step == 0)
    def _():
        small_ref[...] = jnp.zeros_like(small_ref)

    @pl.when(step < BLOCKS)
    def _():
        back = dot_nt(dq_ref[...], w_ref[0]) + dot_nt(dk_ref[...], w_ref[1]) + dot_nt(dv_ref[...], w_ref[2])
        unit, rstd = normalize(x_ref[...])
        out_ref[...] = mid_g_ref[...] + norm_pull(back, gain_ref[...], unit, rstd)
        small_ref[0:1, :] += jnp.sum(back * unit, axis=0, keepdims=True)
        small_ref[1:2, :] += jnp.sum(back, axis=0, keepdims=True)

    @pl.when(step >= BLOCKS)
    def _():
        out_ref[...] = mid_g_ref[...]


def input_bwd(dq, dk, dv, w, x, gain, mid_g):
    length, width = x.shape
    rows = pl.BlockSpec((BLOCK, width), lambda i: (i, 0))
    live = pl.BlockSpec((BLOCK, width), lambda i: (jnp.minimum(i, BLOCKS - 1), 0))
    whole = lambda *shape: pl.BlockSpec(shape, lambda i: (0,) * len(shape))
    return pl.pallas_call(
        input_bwd_body,
        grid=(length // BLOCK,),
        in_specs=[live, live, live, whole(3, width, width), rows, whole(1, width), rows],
        out_specs=[rows, whole(8, width)],
        out_shape=[jax.ShapeDtypeStruct((length, width), F32), jax.ShapeDtypeStruct((8, width), F32)],
        compiler_params=params_for(48),
        cost_estimate=cost(6 * LIVE * width * width, 1e7),
        name="input_backward",
    )(dq, dk, dv, w, x, gain, mid_g)


def down_grad_body(id_ref, act_ref, g_ref, out_ref):
    me, here = id_ref[0], id_ref[1]
    group, quarters, rows, _ = out_ref.shape
    total = dot_tn(act_ref[...], g_ref[...])
    for part in range(group):
        for quarter in range(quarters):
            out_ref[part ^ (me & (group - 1)), quarter ^ here] = total[part * rows : part * rows + rows, quarter * LANES : quarter * LANES + LANES]


def down_grad(ids, act, g_low, parts, quarters):
    length, hidden = act.shape
    width = g_low.shape[1]
    steps = 4
    group = parts // steps
    rows = hidden // parts
    return pl.pallas_call(
        down_grad_body,
        grid_spec=pltpu.PrefetchScalarGridSpec(
            num_scalar_prefetch=1,
            grid=(steps,),
            in_specs=[
                pl.BlockSpec((length, hidden // steps), lambda i, ids: (0, i)),
                pl.BlockSpec((length, width), lambda i, ids: (0, 0)),
            ],
            out_specs=pl.BlockSpec((group, quarters, rows, LANES), lambda i, ids: (i ^ (ids[0] // group), 0, 0, 0)),
        ),
        out_shape=jax.ShapeDtypeStruct((parts, quarters, rows, LANES), F32),
        compiler_params=params_for(48),
        cost_estimate=cost(2 * length * hidden * width, 1e7),
        name="down_gradient",
    )(ids, act, g_low)


def up_grad_body(id_ref, normed_ref, pre_ref, out_ref):
    me = id_ref[0]
    parts, _, rows, _ = out_ref.shape
    total = dot_tn(normed_ref[...], pre_ref[...])
    per_tile = total.shape[0] // rows
    for part in range(parts):
        tile, first = part // per_tile, (part % per_tile) * rows
        out_ref[part ^ me, 0] = total[first : first + rows, tile * LANES : tile * LANES + LANES]


def up_grad(ids, normed, pre_low, parts, quarters):
    length, hidden = pre_low.shape
    width = normed.shape[1]
    rows = width * (hidden // quarters // LANES) // parts
    return pl.pallas_call(
        up_grad_body,
        grid_spec=pltpu.PrefetchScalarGridSpec(
            num_scalar_prefetch=1,
            grid=(quarters,),
            in_specs=[
                pl.BlockSpec((length, width), lambda i, ids: (0, 0)),
                pl.BlockSpec((length, hidden // quarters), lambda i, ids: (0, i)),
            ],
            out_specs=pl.BlockSpec((parts, 1, rows, LANES), lambda i, ids: (0, i ^ ids[1], 0, 0)),
        ),
        out_shape=jax.ShapeDtypeStruct((parts, quarters, rows, LANES), F32),
        compiler_params=params_for(48),
        cost_estimate=cost(2 * length * hidden * width, 1e7),
        name="up_gradient",
    )(ids, normed, pre_low)


def square_grad_body(id_ref, left_ref, *refs):
    right_refs, out_ref = refs[:-1], refs[-1]
    me, here = id_ref[0], id_ref[1]
    parts, quarters, rows, _ = out_ref.shape
    for which, right_ref in enumerate(right_refs):
        total = dot_tn(left_ref[...], right_ref[...])
        unit = math.gcd(total.shape[0], rows)
        for first in range(0, total.shape[0], unit):
            part, offset = divmod(which * total.shape[0] + first, rows)
            for quarter in range(quarters):
                out_ref[part ^ me, quarter ^ here, offset : offset + unit, :] = total[first : first + unit, quarter * LANES : quarter * LANES + LANES]


def square_grad(ids, left, rights, parts, quarters, name):
    length, width = left.shape
    rows = len(rights) * width // parts
    whole = pl.BlockSpec((length, width), lambda i, ids: (0, 0))
    return pl.pallas_call(
        square_grad_body,
        grid_spec=pltpu.PrefetchScalarGridSpec(
            num_scalar_prefetch=1,
            grid=(1,),
            in_specs=[whole] * (1 + len(rights)),
            out_specs=pl.BlockSpec((parts, quarters, rows, LANES), lambda i, ids: (0, 0, 0, 0)),
        ),
        out_shape=jax.ShapeDtypeStruct((parts, quarters, rows, LANES), F32),
        compiler_params=params_for(48),
        cost_estimate=cost(2 * length * width * width * len(rights), 6e6),
        name=name,
    )(ids, left, *rights)


def forward_layer(x, weights, fm, lengths):
    gains, shifts, w, wo, up, up_bias, down, down_bias = weights
    normed, phi_q, phi_k, uq, uk, v, att, rden, low = attn_fwd(lengths, x, gains[0:1], shifts[0:1], w, fm)
    out, mid, normed_two, act, slope = ff_fwd(x, low, wo, gains[1:2], shifts[1:2], up, up_bias[None], down, down_bias[None])
    return out, (x, normed, phi_q, phi_k, uq, uk, v, att, rden, low, mid, normed_two, act, slope)


def backward_layer(grad, kept, weights, fm, lengths, ids, parts, quarters, emit):
    gains, shifts, w, wo, up, up_bias, down, down_bias = weights
    x, normed, phi_q, phi_k, uq, uk, v, att, rden, low, mid, normed_two, act, slope = kept
    g_low, pre_low, mid_g, mid_low, att_g, small_two, up_bias_g = ff_bwd(grad, slope, mid, gains[1:2], up, down, wo)
    emit("down", down_grad(ids, act, g_low, parts, quarters))
    emit("up", up_grad(ids, normed_two, pre_low, parts, quarters))
    emit("out", square_grad(ids, low, [mid_low[:LIVE]], parts, quarters, "out_gradient"))
    dq, dk, dv = attn_bwd(lengths, att_g, att, rden, phi_q, phi_k, uq, uk, v, fm)
    emit("qkv", square_grad(ids, normed, [dq, dk, dv], parts, quarters, "qkv_gradient"))
    grad_in, small_one = input_bwd(dq, dk, dv, w, x, gains[0:1], mid_g)
    smalls = jnp.concatenate([small_one[0], small_two[0], small_one[1], small_two[1], up_bias_g[0], small_two[2]])
    return grad_in, smalls


def swap(block, axis_name, bit):
    return lax.ppermute(block, axis_name, [(i, i ^ bit) for i in range(lax.axis_size(axis_name))])


def halve(block, names, order, axis_name):
    names = list(names)
    for bit in order:
        where = names.index(bit)
        kept = lax.index_in_dim(block, 0, where, keepdims=False)
        block = kept + swap(lax.index_in_dim(block, 1, where, keepdims=False), axis_name, bit)
        names.remove(bit)
    return block


def double(block, names, order, axis_name):
    names_now = []
    for bit in reversed(order):
        names_now.append(bit)
        names_now.sort(key=names.index)
        block = jnp.stack([block, swap(block, axis_name, bit)], axis=names_now.index(bit))
    return block


def bits_of(extent):
    return [1 << i for i in range(extent.bit_length() - 1)]


def exchange(block):
    parts, quarters, rows, _ = block.shape
    dp_bits, batch_bits = bits_of(parts), bits_of(quarters)
    near, far = dp_bits[0], dp_bits[1:]
    block = block.reshape((2,) * len(dp_bits) + block.shape[1:])
    block = halve(block, dp_bits, [near], "dp")
    half = rows // 2
    upper = halve(block[..., :half, :], far, far, "dp")
    lower = halve(block[..., half:, :], far, far[::-1], "dp")
    block = jnp.concatenate([upper, lower], axis=-2)
    block = block.reshape((2,) * len(batch_bits) + block.shape[1:])
    block = halve(block, batch_bits[::-1], batch_bits, "batch")
    upper = double(block[:half], far, far, "dp")
    lower = double(block[half:], far, far[::-1], "dp")
    block = jnp.concatenate([upper, lower], axis=-2)
    block = double(block[None], [near], [near], "dp") if not far else jnp.stack([block, swap(block, "dp", near)])
    return block.reshape(parts, rows, LANES)


def unpack_body(id_ref, *refs):
    count = len(refs) // 2
    for which in range(count):
        refs[count + which][...] = refs[which][...].reshape(refs[count + which].shape)


def unpack(ids, pieces, width, quarter_hidden):
    parts = pieces[0]["qkv"].shape[0]
    layers = len(pieces)
    names = ("qkv", "out", "up", "down")
    arrays, in_specs, out_specs, out_shape = [], [], [], []
    for layer in range(layers):
        for name in names:
            array = pieces[layer][name]
            arrays.append(array)
            in_specs.append(pl.BlockSpec((1,) + array.shape[1:], lambda i, ids: (i ^ ids[0], 0, 0)))
            rows = array.shape[1]
            if name == "up":
                per_tile = width // rows
                out_specs.append(pl.BlockSpec((rows, LANES), lambda i, ids, per_tile=per_tile: (i % per_tile, i // per_tile)))
                out_shape.append(jax.ShapeDtypeStruct((width, quarter_hidden), F32))
            else:
                out_specs.append(pl.BlockSpec((rows, LANES), lambda i, ids: (i, 0)))
                out_shape.append(jax.ShapeDtypeStruct((rows * parts, LANES), F32))
    got = pl.pallas_call(
        unpack_body,
        grid_spec=pltpu.PrefetchScalarGridSpec(num_scalar_prefetch=1, grid=(parts,), in_specs=in_specs, out_specs=out_specs),
        out_shape=out_shape,
        compiler_params=params_for(48),
        cost_estimate=cost(0, 2 * sum(a.size * 4 for a in arrays)),
        name="unpack",
    )(ids, *arrays)
    return [jnp.stack([got[layer * len(names) + which] for layer in range(layers)]) for which in range(len(names))]


def reverse_bits(value, extent):
    bits = bits_of(extent)
    return sum(((value // bit) % 2) * (extent // (2 * bit)) for bit in bits)


def per_device(activations_in, gains, shifts, qkv_weights, out_weights, up_weights, up_bias, down_weights, down_bias, feature_maps, lengths, cotangent):
    layers, _, width = gains.shape
    hidden = up_bias.shape[1]
    parts, quarters = lax.axis_size("dp"), lax.axis_size("batch")
    here = lax.axis_index("batch")
    ids = jnp.stack([reverse_bits(lax.axis_index("dp"), parts), here]).astype(jnp.int32)
    params = (gains, shifts, qkv_weights, out_weights, up_weights, up_bias, down_weights, down_bias)
    weights = [tuple(param[layer] for param in params) for layer in range(layers)]
    proteins = lengths[0]
    values, kept = activations_in[0], []
    for layer in range(layers):
        values, saved = forward_layer(values, weights[layer], feature_maps[layer], proteins)
        kept.append(saved)
    grad, smalls, pieces = cotangent[0], [None] * layers, [{} for _ in range(layers)]
    for layer in reversed(range(layers)):
        def emit(name, block, layer=layer):
            pieces[layer][name] = exchange(block)

        grad, smalls[layer] = backward_layer(grad, kept[layer], weights[layer], feature_maps[layer], proteins, ids, parts, quarters, emit)
    small = lax.psum(jnp.stack(smalls), ("dp", "batch"))

    def own(first, *lead):
        count = math.prod(lead)
        piece = small[:, first : first + count].reshape((layers,) + lead[:-1] + (quarters, lead[-1] // quarters))
        return lax.dynamic_index_in_dim(piece, here, axis=piece.ndim - 2, keepdims=False)

    qkv, out, up, down = unpack(ids, pieces, width, hidden // quarters)
    return (
        values[None],
        grad[None],
        own(0, 2, width),
        own(2 * width, 2, width),
        qkv.reshape(layers, 3, width, LANES),
        out,
        up,
        own(4 * width, hidden),
        down,
        own(4 * width + hidden, width),
    )


def solution(mesh):
    rows = P(("dp", "batch"), None, None)
    return jax.shard_map(
        per_device,
        mesh=mesh,
        in_specs=(rows,) + (P(),) * 9 + (P(("dp", "batch"), None), rows),
        out_specs=(
            rows,
            rows,
            P(None, None, "batch"),
            P(None, None, "batch"),
            P(None, None, None, "batch"),
            P(None, None, "batch"),
            P(None, None, "batch"),
            P(None, "batch"),
            P(None, None, "batch"),
            P(None, "batch"),
        ),
        check_vma=False,
    )
```

time: 2420 us -> 532 us (0.22)
  waiting for transfers between devices: 922 us -> 118 us
  matrix products: 641 us -> 0 us
  local copies, waits for them, and re-layouts: 542 us -> 62.7 us
  other arithmetic: 221 us -> 16.2 us
  Pallas kernels: 0 us -> 184 us
  starting transfers between devices: 0.08 us -> 95.1 us
  loops' own time: 66.7 us -> 0 us
  blocking collectives: 0 us -> 42.3 us
    unnamed x3 -> x0, waiting for transfers between devices: 837 us -> none
    dot_general x176 -> x0, matrix products: 641 us -> none  [the longest x32 114 us: advance(): jnp.einsum('thm,shm->hts', feat_q, feat_k, precision=highest)]
    pallas_call x0 -> x19, Pallas kernels: none -> 184 us  [the longest x2 49 us: attn_bwd(): pl.pallas_call(attn_bwd_body, grid_spec=pltpu.PrefetchScalarGridSpec(num_...]
    dynamic_update_slice x40 -> x0, local copies, waits for them, and re-layouts: 159 us -> none  [favor_row(): lax.scan(jax.checkpoint(advance), start, (phi_q, phi_k, value_blocks, seg...]
    squeeze x51 -> x63, local copies, waits for them, and re-layouts: 137 us -> 17.5 us  [the longest x4 9.17 us: per_device(): param[layer]]
    ppermute x0 -> x96, waiting for transfers between devices: none -> 118 us  [swap(): lax.ppermute(block, axis_name, [(i, i ^ bit) for i in range(lax.axis_size...]
    ppermute x0 -> x96, starting transfers between devices: none -> 95.1 us  [swap(): lax.ppermute(block, axis_name, [(i, i ^ bit) for i in range(lax.axis_size...]
    psum x1 -> x0, waiting for transfers between devices: 85.6 us -> none  [total_sum(): summed = lax.psum(quarter, 'dp')]
  transfers between devices with their start and end apart: 2 -> 96, of which waited for: 2 -> 54; matrix products, arithmetic and copies ran while one was open for 1% -> 7% of each run, Pallas kernels for 0% -> 6%
where the time goes in v1:
time: 532 us; the launch traced here: 522 us
  Pallas kernels  184 us (35%)
  waiting for transfers between devices  118 us (22%)
  starting transfers between devices  95.1 us (18%)
  local copies, waits for them, and re-layouts  62.7 us (12%)
  blocking collectives  42.3 us (8%)
  other arithmetic  16.2 us (3%)
    ppermute x96, waiting for transfers between devices, swap(): lax.ppermute(block, axis_name, [(i, i ^ bit) for i in range(lax.axis_size...  118 us
    ppermute x96, starting transfers between devices, swap(): lax.ppermute(block, axis_name, [(i, i ^ bit) for i in range(lax.axis_size...  95.1 us
    pallas_call x2, Pallas kernels, attn_bwd(): pl.pallas_call(attn_bwd_body, grid_spec=pltpu.PrefetchScalarGridSpec(num_...  49 us
    psum x1, blocking collectives, per_device(): small = lax.psum(jnp.stack(smalls), ('dp', 'batch'))  42.3 us
    pallas_call x2, Pallas kernels, attn_fwd(): pl.pallas_call(attn_fwd_body, grid_spec=pltpu.PrefetchScalarGridSpec(num_...  32 us
    pallas_call x2, Pallas kernels, ff_fwd(): pl.pallas_call(ff_fwd_body, grid=(length // BLOCK,), in_specs=[rows(width...  28.2 us
    pallas_call x2, Pallas kernels, ff_bwd(): pl.pallas_call(ff_bwd_body, grid=(length // BLOCK,), in_specs=[rows(width...  27.1 us
    unnamed x94, local copies, waits for them, and re-layouts  24.4 us
  transfers between devices with their start and end apart: 96, of which 54 were waited for; matrix products, arithmetic and copies ran while one was open for 7% of the time, Pallas kernels for 6%

profile of v1, /device:TPU:0, one launch (start us, length us, event | category | flops | bytes accessed | tf_op | source)
XLA Modules:
  0.0 521.7 jit_solution(3636854594012367127)
XLA Ops:
  0.7 4.1 slice_bitcast_fusion.4
  12.4 16.0 %attn_forward.2 = (bf16[768,512]{1,0:T(8,128)(2,1)S(1)}, bf16[8,768,256]{2,1,0:T(8,128)(2,1)}, bf16[8,768,256]{2,1,0:T(8,128)(2,1)}, f32[4,768,128]{2,1,0:T(8,12...) custom-call(s32[6]{0:T(128)S(1)} %bitcast.574, ...), custom_call_target="tpu_custom_call" | custom-call | flops 12000000000 | bytes 20000000 | tf_op jit(solution)/shard_map/attn_forward/pallas_call | solution.py:157
  31.5 14.1 %ff_forward.2 = (f32[1024,512]{1,0:T(8,128)S(1)}, f32[1024,512]{1,0:T(8,128)}, bf16[1024,512]{1,0:T(8,128)(2,1)S(1)}, bf16[1024,2048]{1,0:T(8,128)(2,1)}, f32[1024,2048]{1,0:T(8,128)}) custom-call(f32[1024,512]{1,0:T(8,128)} %bitcast.563, bf16[768,512]{1,0:T(8,128)(2,1)S(1)} %get-tuple-element.70.low_ref.left_ref, ...), custom_call_target="tpu_custom_call" | custom-call | flops 4831838208 | bytes 30000000 | tf_op jit(solution)/shard_map/ff_forward/pallas_call | solution.py:235
  46.9 16.0 %attn_forward.3 = (bf16[768,512]{1,0:T(8,128)(2,1)S(1)}, bf16[8,768,256]{2,1,0:T(8,128)(2,1)}, bf16[8,768,256]{2,1,0:T(8,128)(2,1)}, f32[4,768,128]{2,1,0:T(8,12...) custom-call(s32[6]{0:T(128)S(1)} %bitcast.575, ...), custom_call_target="tpu_custom_call" | custom-call | flops 12000000000 | bytes 20000000 | tf_op jit(solution)/shard_map/attn_forward/pallas_call | solution.py:157
  65.3 14.1 %ff_forward.3 = (f32[1024,512]{1,0:T(8,128)}, f32[1024,512]{1,0:T(8,128)S(1)}, bf16[1024,512]{1,0:T(8,128)(2,1)S(1)}, bf16[1024,2048]{1,0:T(8,128)(2,1)}, f32[1024,2048]{1,0:T(8,128)}) custom-call(f32[1024,512]{1,0:T(8,128)} %copy-done.5, bf16[768,512]{1,0:T(8,128)(2,1)S(1)} %get-tuple-element.72.low_ref.left_ref, ...), custom_call_target="tpu_custom_call" | custom-call | flops 4831838208 | bytes 30000000 | tf_op jit(solution)/shard_map/ff_forward/pallas_call | solution.py:235
  81.6 13.6 %ff_backward.2 = (bf16[1024,512]{1,0:T(8,128)(2,1)S(1)}, bf16[1024,2048]{1,0:T(8,128)(2,1)}, f32[1024,512]{1,0:T(8,128)}, bf16[1024,512]{1,0:T(8,128)(2,1)S(1)},...) custom-call(f32[1024,512]{1,0:T(8,128)} %bitcast.670, ...), custom_call_target="tpu_custom_call" | custom-call | flops 4831838208 | bytes 30000000 | tf_op jit(solution)/shard_map/ff_backward/pallas_call | solution.py:302
  97.2 19.5 %attn_backward.2 = (bf16[768,512]{1,0:T(8,128)(2,1)S(1)}, bf16[768,512]{1,0:T(8,128)(2,1)S(1)}, bf16[768,512]{1,0:T(8,128)(2,1)S(1)}) custom-call(s32[6]{0:T(128)S(1)} %bitcast.576, f32[768,512]{1,0:T(8,128)S(1)} %get-tuple-element.76.att_g_ref, f32[4,768,128]{2,1,0:T(8,128)} %get-tuple-element.77.att_ref, f32[4,768,128]{2,1,0:T(8,128)} %get-tuple-element.78.rden_ref, ...), custom_call_target="tpu_custom_call" | custom-call | flops 30000001024 | bytes 20000000 | tf_op jit(solution)/shard_map/attn_backward/pallas_call | solution.py:412
  116.7 4.2 input_backward.2
  122.2 13.4 %ff_backward.3 = (bf16[1024,512]{1,0:T(8,128)(2,1)S(1)}, bf16[1024,2048]{1,0:T(8,128)(2,1)}, f32[1024,512]{1,0:T(8,128)}, bf16[1024,512]{1,0:T(8,128)(2,1)S(1)},...) custom-call(f32[1024,512]{1,0:T(8,128)} %copy-done.14, ...), custom_call_target="tpu_custom_call" | custom-call | flops 4831838208 | bytes 30000000 | tf_op jit(solution)/shard_map/ff_backward/pallas_call | solution.py:302
  136.7 29.5 %attn_backward.3 = (bf16[768,512]{1,0:T(8,128)(2,1)S(1)}, bf16[768,512]{1,0:T(8,128)(2,1)S(1)}, bf16[768,512]{1,0:T(8,128)(2,1)S(1)}) custom-call(s32[6]{0:T(128)S(1)} %bitcast.577, f32[768,512]{1,0:T(8,128)S(1)} %get-tuple-element.91.att_g_ref, f32[4,768,128]{2,1,0:T(8,128)} %get-tuple-element.92.att_ref, f32[4,768,128]{2,1,0:T(8,128)} %get-tuple-element.93.rden_ref, ...), custom_call_target="tpu_custom_call" | custom-call | flops 30000001024 | bytes 20000000 | tf_op jit(solution)/shard_map/attn_backward/pallas_call | solution.py:412
  166.2 3.6 qkv_gradient.2
  169.9 3.3 fusion.77
  177.9 5.7 %up_gradient.2 = f32[8,4,256,128]{3,2,1,0:T(8,128)S(1)} custom-call(s32[2]{0:T(128)S(1)} %pad_add_fusion.id_ref, bf16[1024,512]{1,0:T(8,128)(2,1)S(1)} %get-tuple-element.112.normed_ref, bf16[1024,2048]{1,0:T(8,128)(2,1)} %get-tuple-element.113.pre_ref), custom_call_target="tpu_custom_call" | custom-call | flops 2147483648 | bytes 10000000 | tf_op jit(solution)/shard_map/up_gradient/pallas_call | solution.py:525
  187.4 3.6 qkv_gradient.3
  191.0 3.3 fusion.76
  201.8 4.8 input_backward.3
  206.9 42.3 %psum.7 = f32[2,4608]{1,0:T(2,128)S(1)} all-reduce(f32[2,4608]{1,0:T(2,128)S(1)} %pad_maximum_fusion.32), channel_id=1, replica_groups=mesh['dp'=8,'batch'=4] {'dp','batch'}, use_global_device_ids=true, to_apply=%region_0.1 | all-reduce | flops 9216 | bytes 73728 | tf_op jit(solution)/shard_map/psum | solution.py:701
  250.5 5.4 %down_gradient.2 = f32[8,4,256,128]{3,2,1,0:T(8,128)S(1)} custom-call(s32[2]{0:T(128)S(1)} %pad_add_fusion.id_ref, bf16[1024,2048]{1,0:T(8,128)(2,1)} %get-tuple-element.114.act_ref, bf16[1024,512]{1,0:T(8,128)(2,1)S(1)} %copy-done.11), custom_call_target="tpu_custom_call" | custom-call | flops 2147483648 | bytes 10000000 | tf_op jit(solution)/shard_map/down_gradient/pallas_call | solution.py:493
  258.5 5.7 %up_gradient.3 = f32[8,4,256,128]{3,2,1,0:T(8,128)S(1)} custom-call(s32[2]{0:T(128)S(1)} %pad_add_fusion.id_ref, bf16[1024,512]{1,0:T(8,128)(2,1)S(1)} %copy-done.9, bf16[1024,2048]{1,0:T(8,128)(2,1)} %get-tuple-element.119.pre_ref), custom_call_target="tpu_custom_call" | custom-call | flops 2147483648 | bytes 10000000 | tf_op jit(solution)/shard_map/up_gradient/pallas_call | solution.py:525
  266.5 5.6 %down_gradient.3 = f32[8,4,256,128]{3,2,1,0:T(8,128)S(1)} custom-call(s32[2]{0:T(128)S(1)} %pad_add_fusion.id_ref, bf16[1024,2048]{1,0:T(8,128)(2,1)} %get-tuple-element.120.act_ref, bf16[1024,512]{1,0:T(8,128)(2,1)S(1)} %copy-done.7), custom_call_target="tpu_custom_call" | custom-call | flops 2147483648 | bytes 10000000 | tf_op jit(solution)/shard_map/down_gradient/pallas_call | solution.py:493
  283.4 3.2 collective-permute-done.61
  332.1 7.8 %collective-permute-done.1 = f32[2,4,96,128]{3,2,1,0:T(8,128)S(1)} collective-permute-done((f32[2,4,96,128]{3,2,1,0:T(8,128)S(1)}, f32[2,4,96,128]{3,2,1,0:T(8,128)S(1)}, u32[]{:S(2)}, u32[]{:S(2)}) %collective-permute-start.1) | collective-permute-done | bytes 393248 | tf_op jit(solution)/shard_map/ppermute | solution.py:597
  342.2 8.5 %collective-permute-done.49 = f32[2,4,96,128]{3,2,1,0:T(8,128)S(1)} collective-permute-done((f32[2,4,96,128]{3,2,1,0:T(8,128)S(1)}, f32[2,4,96,128]{3,2,1,0:T(8,128)S(1)}, u32[]{:S(2)}, u32[]{:S(2)}) %collective-permute-start.49) | collective-permute-done | bytes 393248 | tf_op jit(solution)/shard_map/ppermute | solution.py:597
  366.5 4.6 collective-permute-done.5
  382.2 3.6 collective-permute-done.9
  407.6 7.4 %collective-permute-done.39 = f32[2,4,128,128]{3,2,1,0:T(8,128)S(1)} collective-permute-done((f32[2,4,128,128]{3,2,1,0:T(8,128)S(1)}, f32[2,4,128,128]{3,2,1,0:T(8,128)S(1)}, u32[]{:S(2)}, u32[]{:S(2)}) %collective-permute-start.39) | collective-permute-done | bytes 524320 | tf_op jit(solution)/shard_map/ppermute | solution.py:597
  418.1 8.2 %collective-permute-done.75 = f32[2,4,128,128]{3,2,1,0:T(8,128)S(1)} collective-permute-done((f32[2,4,128,128]{3,2,1,0:T(8,128)S(1)}, f32[2,4,128,128]{3,2,1,0:T(8,128)S(1)}, u32[]{:S(2)}, u32[]{:S(2)}) %collective-permute-start.75) | collective-permute-done | bytes 524320 | tf_op jit(solution)/shard_map/ppermute | solution.py:597
  428.7 8.8 %collective-permute-done.87 = f32[2,4,128,128]{3,2,1,0:T(8,128)S(1)} collective-permute-done((f32[2,4,128,128]{3,2,1,0:T(8,128)S(1)}, f32[2,4,128,128]{3,2,1,0:T(8,128)S(1)}, u32[]{:S(2)}, u32[]{:S(2)}) %collective-permute-start.87) | collective-permute-done | bytes 524320 | tf_op jit(solution)/shard_map/ppermute | solution.py:597
  445.5 3.3 collective-permute-done.38
  456.4 7.0 %collective-permute-done.29 = f32[2,256,128]{2,1,0:T(8,128)S(1)} collective-permute-done((f32[2,256,128]{2,1,0:T(8,128)S(1)}, f32[2,256,128]{2,1,0:T(8,128)S(1)}, u32[]{:S(2)}, u32[]{:S(2)}) %collective-permute-start.29) | collective-permute-done | bytes 262176 | tf_op jit(solution)/shard_map/ppermute | solution.py:597
  466.5 6.7 %collective-permute-done.77 = f32[2,256,128]{2,1,0:T(8,128)S(1)} collective-permute-done((f32[2,256,128]{2,1,0:T(8,128)S(1)}, f32[2,256,128]{2,1,0:T(8,128)S(1)}, u32[]{:S(2)}, u32[]{:S(2)}) %collective-permute-start.77) | collective-permute-done | bytes 262176 | tf_op jit(solution)/shard_map/ppermute | solution.py:597
  508.3 7.1 %unpack.1 = (f32[1536,128]{1,0:T(8,128)S(1)}, f32[512,128]{1,0:T(8,128)S(1)}, f32[512,512]{1,0:T(8,128)S(1)}, f32[2048,128]{1,0:T(8,128)}, f32[1536,128]{1,0:T(8...) custom-call(s32[2]{0:T(128)S(1)} %pad_add_fusion.id_ref, ...), custom_call_target="tpu_custom_call" | custom-call | bytes 12582912 | tf_op jit(solution)/shard_map/unpack/pallas_call | solution.py:666
  (477 shorter events, 214.6 us)
Async XLA Ops:
  174.5 151.2 %collective-permute-start = (f32[2,2,4,192,128]{4,3,2,0,1:T(8,128)}, f32[2,2,4,192,128]{4,3,2,0,1:T(8,128)}, u32[]{:S(2)}, u32[]{:S(2)}) collective-permute-start(f32[2,2,4,192,128]{4,3,2,0,1:T(8,128)} %copy.38), channel_id=1, source_target_pairs={{0,4},{4,0},{8,12},{12,8},{16,20},{20,16},{24,28},{28,24},{1,5},{5... | collective-permute-start | bytes 4718600 | tf_op jit(solution)/shard_map/ppermute | solution.py:597
  177.9 95.7 %collective-permute-start.12 = (f32[2,2,4,64,128]{4,3,2,0,1:T(8,128)}, f32[2,2,4,64,128]{4,3,2,0,1:T(8,128)}, u32[]{:S(2)}, u32[]{:S(2)}) collective-permute-start(f32[2,2,4,64,128]{4,3,2,0,1:T(8,128)} %copy.44), channel_id=1, source_target_pairs={{0,4},{4,0},{8,12},{12,8},{16,20},{20,16},{24,28},{28,24},{1,5},{5... | collective-permute-start | bytes 1572872 | tf_op jit(solution)/shard_map/ppermute | solution.py:597
  186.9 165.8 %collective-permute-start.24 = (f32[2,2,4,256,128]{4,3,2,0,1:T(8,128)}, f32[2,2,4,256,128]{4,3,2,0,1:T(8,128)}, u32[]{:S(2)}, u32[]{:S(2)}) collective-permute-start(f32[2,2,4,256,128]{4,3,2,0,1:T(8,128)} %copy.50), channel_id=1, source_target_pairs={{0,4},{4,0},{8,12},{12,8},{16,20},{20,16},{24,28},{28,24},{1,5},{5... | collective-permute-start | bytes 6291464 | tf_op jit(solution)/shard_map/ppermute | solution.py:597
  195.6 134.5 %collective-permute-start.48 = (f32[2,2,4,192,128]{4,3,2,0,1:T(8,128)}, f32[2,2,4,192,128]{4,3,2,0,1:T(8,128)}, u32[]{:S(2)}, u32[]{:S(2)}) collective-permute-start(f32[2,2,4,192,128]{4,3,2,0,1:T(8,128)} %copy.62), channel_id=1, source_target_pairs={{0,4},{4,0},{8,12},{12,8},{16,20},{20,16},{24,28},{28,24},{1,5},{5... | collective-permute-start | bytes 4718600 | tf_op jit(solution)/shard_map/ppermute | solution.py:597
  199.0 78.7 %collective-permute-start.60 = (f32[2,2,4,64,128]{4,3,2,0,1:T(8,128)}, f32[2,2,4,64,128]{4,3,2,0,1:T(8,128)}, u32[]{:S(2)}, u32[]{:S(2)}) collective-permute-start(f32[2,2,4,64,128]{4,3,2,0,1:T(8,128)} %copy.68), channel_id=1, source_target_pairs={{0,4},{4,0},{8,12},{12,8},{16,20},{20,16},{24,28},{28,24},{1,5},{5... | collective-permute-start | bytes 1572872 | tf_op jit(solution)/shard_map/ppermute | solution.py:597
  324.9 31.5 %collective-permute-start.36 = (f32[2,2,4,256,128]{4,3,2,0,1:T(8,128)S(1)}, f32[2,2,4,256,128]{4,3,2,0,1:T(8,128)S(1)}, u32[]{:S(2)}, u32[]{:S(2)}) collective-permute-start(f32[2,2,4,256,128]{4,3,2,0,1:T(8,128)S(1)} %copy.56), channel_id=1, source_target_pairs={{0,4},{4,0},{8,12},{12,8},{16,20},{20,16},{24,28},{28,24},{1,5},{5... | collective-permute-start | bytes 6291464 | tf_op jit(solution)/shard_map/ppermute | solution.py:597
  325.5 32.7 %collective-permute-start.72 = (f32[2,2,4,256,128]{4,3,2,0,1:T(8,128)S(1)}, f32[2,2,4,256,128]{4,3,2,0,1:T(8,128)S(1)}, u32[]{:S(2)}, u32[]{:S(2)}) collective-permute-start(f32[2,2,4,256,128]{4,3,2,0,1:T(8,128)S(1)} %copy.74), channel_id=1, source_target_pairs={{0,4},{4,0},{8,12},{12,8},{16,20},{20,16},{24,28},{28,24},{1,5},{5... | collective-permute-start | bytes 6291464 | tf_op jit(solution)/shard_map/ppermute | solution.py:597
  328.1 11.8 %collective-permute-start.1 = (f32[2,4,96,128]{3,2,1,0:T(8,128)S(1)}, f32[2,4,96,128]{3,2,1,0:T(8,128)S(1)}, u32[]{:S(2)}, u32[]{:S(2)}) collective-permute-start(f32[2,4,96,128]{3,2,1,0:T(8,128)S(1)} %slice_bitcast_fusion.32), channel_id=1, source_target_pairs={{0,8},{4,12},{8,0},{12,4},{16,24},{20,28},{24,16},{28,20},{1,9},{5... | collective-permute-start | bytes 1179656 | tf_op jit(solution)/shard_map/ppermute | solution.py:597
  330.1 11.5 %collective-permute-start.3 = (f32[2,4,96,128]{3,2,1,0:T(8,128)S(1)}, f32[2,4,96,128]{3,2,1,0:T(8,128)S(1)}, u32[]{:S(2)}, u32[]{:S(2)}) collective-permute-start(f32[2,4,96,128]{3,2,1,0:T(8,128)S(1)} %slice_bitcast_fusion.30), channel_id=1, source_target_pairs={{0,16},{4,20},{8,24},{12,28},{16,0},{20,4},{24,8},{28,12},{1,17},{... | collective-permute-start | bytes 1179656 | tf_op jit(solution)/shard_map/ppermute | solution.py:597
  339.9 10.8 %collective-permute-start.49 = (f32[2,4,96,128]{3,2,1,0:T(8,128)S(1)}, f32[2,4,96,128]{3,2,1,0:T(8,128)S(1)}, u32[]{:S(2)}, u32[]{:S(2)}) collective-permute-start(f32[2,4,96,128]{3,2,1,0:T(8,128)S(1)} %slice_bitcast_fusion.28), channel_id=1, source_target_pairs={{0,8},{4,12},{8,0},{12,4},{16,24},{20,28},{24,16},{28,20},{1,9},{5... | collective-permute-start | bytes 1179656 | tf_op jit(solution)/shard_map/ppermute | solution.py:597
  341.6 10.4 %collective-permute-start.51 = (f32[2,4,96,128]{3,2,1,0:T(8,128)S(1)}, f32[2,4,96,128]{3,2,1,0:T(8,128)S(1)}, u32[]{:S(2)}, u32[]{:S(2)}) collective-permute-start(f32[2,4,96,128]{3,2,1,0:T(8,128)S(1)} %slice_bitcast_fusion.26), channel_id=1, source_target_pairs={{0,16},{4,20},{8,24},{12,28},{16,0},{20,4},{24,8},{28,12},{1,17},{... | collective-permute-start | bytes 1179656 | tf_op jit(solution)/shard_map/ppermute | solution.py:597
  359.3 44.0 %collective-permute-start.25 = (f32[2,4,128,128]{3,2,1,0:T(8,128)S(1)}, f32[2,4,128,128]{3,2,1,0:T(8,128)S(1)}, u32[]{:S(2)}, u32[]{:S(2)}) collective-permute-start(f32[2,4,128,128]{3,2,1,0:T(8,128)S(1)} %slice_bitcast_fusion.20), channel_id=1, source_target_pairs={{0,8},{4,12},{8,0},{12,4},{16,24},{20,28},{24,16},{28,20},{1,9},{5... | collective-permute-start | bytes 1572872 | tf_op jit(solution)/shard_map/ppermute | solution.py:597
  361.1 44.2 %collective-permute-start.27 = (f32[2,4,128,128]{3,2,1,0:T(8,128)S(1)}, f32[2,4,128,128]{3,2,1,0:T(8,128)S(1)}, u32[]{:S(2)}, u32[]{:S(2)}) collective-permute-start(f32[2,4,128,128]{3,2,1,0:T(8,128)S(1)} %slice_bitcast_fusion.18), channel_id=1, source_target_pairs={{0,16},{4,20},{8,24},{12,28},{16,0},{20,4},{24,8},{28,12},{1,17},{... | collective-permute-start | bytes 1572872 | tf_op jit(solution)/shard_map/ppermute | solution.py:597
  361.9 43.7 %collective-permute-start.37 = (f32[2,4,128,128]{3,2,1,0:T(8,128)S(1)}, f32[2,4,128,128]{3,2,1,0:T(8,128)S(1)}, u32[]{:S(2)}, u32[]{:S(2)}) collective-permute-start(f32[2,4,128,128]{3,2,1,0:T(8,128)S(1)} %slice_bitcast_fusion.16), channel_id=1, source_target_pairs={{0,8},{4,12},{8,0},{12,4},{16,24},{20,28},{24,16},{28,20},{1,9},{5... | collective-permute-start | bytes 1572872 | tf_op jit(solution)/shard_map/ppermute | solution.py:597
  399.9 15.2 %collective-permute-start.39 = (f32[2,4,128,128]{3,2,1,0:T(8,128)S(1)}, f32[2,4,128,128]{3,2,1,0:T(8,128)S(1)}, u32[]{:S(2)}, u32[]{:S(2)}) collective-permute-start(f32[2,4,128,128]{3,2,1,0:T(8,128)S(1)} %slice_bitcast_fusion.14), channel_id=1, source_target_pairs={{0,16},{4,20},{8,24},{12,28},{16,0},{20,4},{24,8},{28,12},{1,17},{... | collective-permute-start | bytes 1572872 | tf_op jit(solution)/shard_map/ppermute | solution.py:597
  403.2 14.9 %collective-permute-start.73 = (f32[2,4,128,128]{3,2,1,0:T(8,128)S(1)}, f32[2,4,128,128]{3,2,1,0:T(8,128)S(1)}, u32[]{:S(2)}, u32[]{:S(2)}) collective-permute-start(f32[2,4,128,128]{3,2,1,0:T(8,128)S(1)} %slice_bitcast_fusion.12), channel_id=1, source_target_pairs={{0,8},{4,12},{8,0},{12,4},{16,24},{20,28},{24,16},{28,20},{1,9},{5... | collective-permute-start | bytes 1572872 | tf_op jit(solution)/shard_map/ppermute | solution.py:597
  403.3 23.0 %collective-permute-start.75 = (f32[2,4,128,128]{3,2,1,0:T(8,128)S(1)}, f32[2,4,128,128]{3,2,1,0:T(8,128)S(1)}, u32[]{:S(2)}, u32[]{:S(2)}) collective-permute-start(f32[2,4,128,128]{3,2,1,0:T(8,128)S(1)} %slice_bitcast_fusion.10), channel_id=1, source_target_pairs={{0,16},{4,20},{8,24},{12,28},{16,0},{20,4},{24,8},{28,12},{1,17},{... | collective-permute-start | bytes 1572872 | tf_op jit(solution)/shard_map/ppermute | solution.py:597
  405.3 23.4 %collective-permute-start.85 = (f32[2,4,128,128]{3,2,1,0:T(8,128)S(1)}, f32[2,4,128,128]{3,2,1,0:T(8,128)S(1)}, u32[]{:S(2)}, u32[]{:S(2)}) collective-permute-start(f32[2,4,128,128]{3,2,1,0:T(8,128)S(1)} %slice_bitcast_fusion.8), channel_id=1, source_target_pairs={{0,8},{4,12},{8,0},{12,4},{16,24},{20,28},{24,16},{28,20},{1,9},{5... | collective-permute-start | bytes 1572872 | tf_op jit(solution)/shard_map/ppermute | solution.py:597
  405.6 31.9 %collective-permute-start.87 = (f32[2,4,128,128]{3,2,1,0:T(8,128)S(1)}, f32[2,4,128,128]{3,2,1,0:T(8,128)S(1)}, u32[]{:S(2)}, u32[]{:S(2)}) collective-permute-start(f32[2,4,128,128]{3,2,1,0:T(8,128)S(1)} %slice_bitcast_fusion.6), channel_id=1, source_target_pairs={{0,16},{4,20},{8,24},{12,28},{16,0},{20,4},{24,8},{28,12},{1,17},{... | collective-permute-start | bytes 1572872 | tf_op jit(solution)/shard_map/ppermute | solution.py:597
  415.1 81.8 %collective-permute-start.11 = (f32[2,2,192,128]{3,2,0,1:T(8,128)S(1)}, f32[2,2,192,128]{3,2,0,1:T(8,128)S(1)}, u32[]{:S(2)}, u32[]{:S(2)}) collective-permute-start(f32[2,2,192,128]{3,2,0,1:T(8,128)S(1)} %get-tuple-element.183), channel_id=1, source_target_pairs={{0,4},{4,0},{8,12},{12,8},{16,20},{20,16},{24,28},{28,24},{1,5},{5... | collective-permute-start | bytes 1179656 | tf_op jit(solution)/shard_map/ppermute | solution.py:597
  418.0 21.7 %collective-permute-start.28 = (f32[4,128,128]{2,1,0:T(8,128)S(1)}, f32[4,128,128]{2,1,0:T(8,128)S(1)}, u32[]{:S(2)}, u32[]{:S(2)}) collective-permute-start(f32[4,128,128]{2,1,0:T(8,128)S(1)} %slice_bitcast_fusion.54), channel_id=1, source_target_pairs={{0,8},{4,12},{8,0},{12,4},{16,24},{20,28},{24,16},{28,20},{1,9},{5... | collective-permute-start | bytes 786440 | tf_op jit(solution)/shard_map/ppermute | solution.py:597
  426.3 16.9 %collective-permute-start.26 = (f32[4,128,128]{2,1,0:T(8,128)S(1)}, f32[4,128,128]{2,1,0:T(8,128)S(1)}, u32[]{:S(2)}, u32[]{:S(2)}) collective-permute-start(f32[4,128,128]{2,1,0:T(8,128)S(1)} %slice_bitcast_fusion.56), channel_id=1, source_target_pairs={{0,16},{4,20},{8,24},{12,28},{16,0},{20,4},{24,8},{28,12},{1,17},{... | collective-permute-start | bytes 786440 | tf_op jit(solution)/shard_map/ppermute | solution.py:597
  428.7 16.5 %collective-permute-start.40 = (f32[4,128,128]{2,1,0:T(8,128)S(1)}, f32[4,128,128]{2,1,0:T(8,128)S(1)}, u32[]{:S(2)}, u32[]{:S(2)}) collective-permute-start(f32[4,128,128]{2,1,0:T(8,128)S(1)} %slice_bitcast_fusion.48), channel_id=1, source_target_pairs={{0,8},{4,12},{8,0},{12,4},{16,24},{20,28},{24,16},{28,20},{1,9},{5... | collective-permute-start | bytes 786440 | tf_op jit(solution)/shard_map/ppermute | solution.py:597
  437.5 11.2 %collective-permute-start.38 = (f32[4,128,128]{2,1,0:T(8,128)S(1)}, f32[4,128,128]{2,1,0:T(8,128)S(1)}, u32[]{:S(2)}, u32[]{:S(2)}) collective-permute-start(f32[4,128,128]{2,1,0:T(8,128)S(1)} %slice_bitcast_fusion.50), channel_id=1, source_target_pairs={{0,16},{4,20},{8,24},{12,28},{16,0},{20,4},{24,8},{28,12},{1,17},{... | collective-permute-start | bytes 786440 | tf_op jit(solution)/shard_map/ppermute | solution.py:597
  439.8 11.1 %collective-permute-start.76 = (f32[4,128,128]{2,1,0:T(8,128)S(1)}, f32[4,128,128]{2,1,0:T(8,128)S(1)}, u32[]{:S(2)}, u32[]{:S(2)}) collective-permute-start(f32[4,128,128]{2,1,0:T(8,128)S(1)} %slice_bitcast_fusion.42), channel_id=1, source_target_pairs={{0,8},{4,12},{8,0},{12,4},{16,24},{20,28},{24,16},{28,20},{1,9},{5... | collective-permute-start | bytes 786440 | tf_op jit(solution)/shard_map/ppermute | solution.py:597
  443.1 9.4 %collective-permute-start.74 = (f32[4,128,128]{2,1,0:T(8,128)S(1)}, f32[4,128,128]{2,1,0:T(8,128)S(1)}, u32[]{:S(2)}, u32[]{:S(2)}) collective-permute-start(f32[4,128,128]{2,1,0:T(8,128)S(1)} %slice_bitcast_fusion.44), channel_id=1, source_target_pairs={{0,16},{4,20},{8,24},{12,28},{16,0},{20,4},{24,8},{28,12},{1,17},{... | collective-permute-start | bytes 786440 | tf_op jit(solution)/shard_map/ppermute | solution.py:597
  450.9 12.5 %collective-permute-start.29 = (f32[2,256,128]{2,1,0:T(8,128)S(1)}, f32[2,256,128]{2,1,0:T(8,128)S(1)}, u32[]{:S(2)}, u32[]{:S(2)}) collective-permute-start(f32[2,256,128]{2,1,0:T(8,128)S(1)} %slice_bitcast_fusion.52), channel_id=1, source_target_pairs={{0,1},{1,0},{2,3},{3,2},{4,5},{5,4},{6,7},{7,6},{8,9},{9,8},{10,11... | collective-permute-start | bytes 786440 | tf_op jit(solution)/shard_map/ppermute | solution.py:597
  452.5 13.7 %collective-permute-start.41 = (f32[2,256,128]{2,1,0:T(8,128)S(1)}, f32[2,256,128]{2,1,0:T(8,128)S(1)}, u32[]{:S(2)}, u32[]{:S(2)}) collective-permute-start(f32[2,256,128]{2,1,0:T(8,128)S(1)} %slice_bitcast_fusion.46), channel_id=1, source_target_pairs={{0,1},{1,0},{2,3},{3,2},{4,5},{5,4},{6,7},{7,6},{8,9},{9,8},{10,11... | collective-permute-start | bytes 786440 | tf_op jit(solution)/shard_map/ppermute | solution.py:597
  453.5 19.7 %collective-permute-start.77 = (f32[2,256,128]{2,1,0:T(8,128)S(1)}, f32[2,256,128]{2,1,0:T(8,128)S(1)}, u32[]{:S(2)}, u32[]{:S(2)}) collective-permute-start(f32[2,256,128]{2,1,0:T(8,128)S(1)} %slice_bitcast_fusion.40), channel_id=1, source_target_pairs={{0,1},{1,0},{2,3},{3,2},{4,5},{5,4},{6,7},{7,6},{8,9},{9,8},{10,11... | collective-permute-start | bytes 786440 | tf_op jit(solution)/shard_map/ppermute | solution.py:597
  455.4 20.6 %collective-permute-start.89 = (f32[2,256,128]{2,1,0:T(8,128)S(1)}, f32[2,256,128]{2,1,0:T(8,128)S(1)}, u32[]{:S(2)}, u32[]{:S(2)}) collective-permute-start(f32[2,256,128]{2,1,0:T(8,128)S(1)} %slice_bitcast_fusion.34), channel_id=1, source_target_pairs={{0,1},{1,0},{2,3},{3,2},{4,5},{5,4},{6,7},{7,6},{8,9},{9,8},{10,11... | collective-permute-start | bytes 786440 | tf_op jit(solution)/shard_map/ppermute | solution.py:597
  463.4 12.9 %collective-permute-start.30 = (f32[256,128]{1,0:T(8,128)S(1)}, f32[256,128]{1,0:T(8,128)S(1)}, u32[]{:S(2)}, u32[]{:S(2)}) collective-permute-start(f32[256,128]{1,0:T(8,128)S(1)} %slice_bitcast_fusion.80), channel_id=1, source_target_pairs={{0,2},{1,3},{2,0},{3,1},{4,6},{5,7},{6,4},{7,5},{8,10},{9,11},{10,... | collective-permute-start | bytes 393224 | tf_op jit(solution)/shard_map/ppermute | solution.py:597
  466.3 11.2 %collective-permute-start.42 = (f32[256,128]{1,0:T(8,128)S(1)}, f32[256,128]{1,0:T(8,128)S(1)}, u32[]{:S(2)}, u32[]{:S(2)}) collective-permute-start(f32[256,128]{1,0:T(8,128)S(1)} %slice_bitcast_fusion.78), channel_id=1, source_target_pairs={{0,2},{1,3},{2,0},{3,1},{4,6},{5,7},{6,4},{7,5},{8,10},{9,11},{10,... | collective-permute-start | bytes 393224 | tf_op jit(solution)/shard_map/ppermute | solution.py:597
  (106 other events, 508.8 us)
